TPU v7x, 32 devices: a whole 2x2x4 slice. The times are simulated.
32 devices in a mesh: seq: 4 (over x, core), tensor: 8 (over z, y).
Axes of the slice: x: 2, y: 2, z: 4, core: 2. Of those that a mesh axis runs over, the one named last changes fastest.
Arguments:
- hidden: bfloat16 [512, 53248], P('seq', 'tensor'), may hold values from -200 to 200, as said below
- down_int: bfloat16 [53248, 16384], P('tensor', 'seq'), may hold values from -8 to 7, as said below
- w_scale: float32 [16384], P('seq'), may hold values from 0.0004 to 0.0025
- had_small: int32 [52, 52], replicated, may hold values from -1 to 1, as said below
Outputs:
- mixed: bfloat16 [512, 16384], P('tensor', 'seq')
- act_scale: float32 [512], P('seq')
Inputs may be any that keep to these rules, and one draw needn't show every extreme that they name: `hidden`: activations with unequal token and channel scales. `down_int`: whole numbers. A Hadamard matrix: entries -1 or +1 and had_small had_small^T = 52 I.
All inputs are finite; a program needn't handle non-finite values.
Results may differ from a plain program's by a relative error of at most 0.0011.
Values may be sent and summed in bfloat16 or wider, within the bound.
A program may use at most 192 MiB of HBM per device.

v0:
```python
import functools
import math

import jax
import jax.numpy as jnp
from jax import lax
from jax.experimental import pallas as pl
from jax.experimental.pallas import tpu as pltpu
from jax.sharding import PartitionSpec as P

BLOCKS = 1024
LANES = 128
ROWS = 8
LAG = 3

clip_ratio = 0.9
epsilon = 1e-05


def parity_sign(left_index, right_index, order):
    both = left_index & right_index
    parity = jnp.zeros(both.shape, jnp.int32)
    for shift_bit in range(max(order.bit_length() - 1, 0)):
        parity = parity ^ ((both >> shift_bit) & 1)
    return 1 - 2 * parity


def inner_factor(had_small, group):
    had = had_small.shape[0]
    width = group * had
    left_index = lax.broadcasted_iota(jnp.int32, (width, had), 0)
    right_index = lax.broadcasted_iota(jnp.int32, (width, had), 1)
    pick = (left_index % had == right_index).astype(jnp.bfloat16)
    tall = jnp.dot(pick, had_small.astype(jnp.bfloat16), preferred_element_type=jnp.float32)
    square = lax.dot_general(
        tall.astype(jnp.bfloat16), pick, (((1,), (1,)), ((), ())), preferred_element_type=jnp.float32
    )
    row_block = lax.broadcasted_iota(jnp.int32, (width, 1), 0) // had
    col_block = lax.broadcasted_iota(jnp.int32, (1, width), 1) // had
    sign = parity_sign(
        jnp.broadcast_to(row_block, (width, width)), jnp.broadcast_to(col_block, (width, width)), group
    )
    return (square * sign.astype(jnp.float32)).astype(jnp.bfloat16)


def rotate_kernel(count, rows, norm_factor, x_ref, k_ref, *rest):
    out_refs, y_ref = rest[:-1], rest[-1]
    width = k_ref.shape[0]
    inner = x_ref.shape[1] // width
    chunks = count * inner
    lane_tiles = width // LANES
    for j in range(inner):
        y_ref[j] = jnp.dot(
            x_ref[:, j * width : (j + 1) * width], k_ref[...], preferred_element_type=jnp.float32
        )
    for h, out_ref in enumerate(out_refs):
        def mix(tile, peak):
            cols = pl.ds(pl.multiple_of(tile * LANES, LANES), LANES)
            vals = [
                y_ref[c % inner, pl.ds((c // inner) * rows + h * ROWS, ROWS), cols] for c in range(chunks)
            ]
            span = 1
            while span < chunks:
                for c in range(chunks):
                    if c & span == 0:
                        vals[c], vals[c + span] = vals[c] + vals[c + span], vals[c] - vals[c + span]
                span *= 2
            for c in range(chunks):
                rotated = vals[c] * norm_factor
                peak = jnp.maximum(peak, jnp.abs(rotated))
                y_ref[c % inner, pl.ds((c // inner) * rows + h * ROWS, ROWS), cols] = rotated
            return peak

        peak = lax.fori_loop(0, lane_tiles, mix, jnp.zeros((ROWS, LANES), jnp.float32))
        peak = jnp.max(peak, axis=1, keepdims=True)
        scale = jnp.broadcast_to(clip_ratio / 7.0 * (peak + epsilon), (ROWS, LANES))
        top = scale.astype(jnp.bfloat16).astype(jnp.float32)
        middle = (scale - top).astype(jnp.bfloat16).astype(jnp.float32)
        lane = lax.broadcasted_iota(jnp.int32, (ROWS, LANES), 1)
        first = jnp.where(lane < LANES // 2, top, scale - top - middle)
        terms = jnp.concatenate([first, middle], axis=0).astype(jnp.bfloat16)
        for i in range(count):
            out_ref[pl.ds(i * 2 * ROWS, 2 * ROWS), pl.ds(inner * width, LANES)] = terms

        def split(tile, carry):
            cols = pl.ds(pl.multiple_of(tile * LANES, LANES), LANES)
            for c in range(chunks):
                rotated = y_ref[c % inner, pl.ds((c // inner) * rows + h * ROWS, ROWS), cols]
                quant = jnp.clip(rotated / scale, -8.0, 7.0)
                high = quant.astype(jnp.bfloat16).astype(jnp.float32)
                both = jnp.concatenate([high, quant - high], axis=0).astype(jnp.bfloat16)
                place = pl.ds(pl.multiple_of((c % inner) * width + tile * LANES, LANES), LANES)
                out_ref[pl.ds((c // inner) * 2 * ROWS, 2 * ROWS), place] = both
            return carry

        lax.fori_loop(0, lane_tiles, split, 0)


def product_kernel(tiles, x_ref, w_ref, gain_ref, out_ref, scale_ref, mine, half, from_pair, from_line, *sems):
    pair_send, pair_recv, line_send, line_recv = sems
    step = pl.program_id(0)
    me = lax.axis_index("tensor")
    parity = me % 2
    place = me // 2
    line = mine.shape[2]
    own = mine.shape[3]
    span = w_ref.shape[1]
    narrow = min(256, span)
    depth = w_ref.shape[0]
    partner = me + 1 - 2 * parity

    def pair_copy(tile):
        return pltpu.make_async_remote_copy(
            src_ref=mine.at[tile, 1 - parity],
            dst_ref=from_pair.at[tile],
            send_sem=pair_send.at[tile],
            recv_sem=pair_recv.at[tile],
            device_id={"tensor": partner},
            device_id_type=pl.DeviceIdType.MESH,
        )

    def line_copy(tile, hop):
        target = (place + hop) % line
        return pltpu.make_async_remote_copy(
            src_ref=half.at[tile, target],
            dst_ref=from_line.at[tile, hop - 1],
            send_sem=line_send.at[tile, hop - 1],
            recv_sem=line_recv.at[tile, hop - 1],
            device_id={"tensor": 2 * target + parity},
            device_id_type=pl.DeviceIdType.MESH,
        )

    @pl.when(step == 0)
    def _():
        barrier = pltpu.get_barrier_semaphore()
        pl.semaphore_signal(
            barrier, inc=1, device_id={"tensor": partner}, device_id_type=pl.DeviceIdType.MESH
        )
        for hop in range(1, line):
            pl.semaphore_signal(
                barrier,
                inc=1,
                device_id={"tensor": 2 * ((place + hop) % line) + parity},
                device_id_type=pl.DeviceIdType.MESH,
            )
        pl.semaphore_wait(barrier, line)
        terms = x_ref[:, depth:].astype(jnp.float32).reshape(-1, 2, ROWS, LANES)
        first = terms[:, 0].reshape(-1, LANES)
        middle = terms[:, 1].reshape(-1, LANES)
        scale_ref[...] = first + middle + pltpu.roll(first, LANES // 2, 1)

    @pl.when(step < tiles)
    def _():
        def piece(n, carry):
            cols = pl.ds(pl.multiple_of(n * narrow, narrow), narrow)
            terms = jnp.dot(x_ref[:, :depth], w_ref[:, cols], preferred_element_type=jnp.float32)
            terms = terms.reshape(-1, 2, ROWS, narrow)
            sums = (terms[:, 0] + terms[:, 1]).reshape(2 * line, own, narrow)
            for owner in range(2 * line):
                mine[step, owner % 2, owner // 2, :, cols] = sums[owner]
            return carry

        lax.fori_loop(0, span // narrow, piece, 0)
        pair_copy(step).start()

    @pl.when((step >= 1) & (step <= tiles))
    def _():
        tile = step - 1
        pair_copy(tile).wait_recv()
        half[tile] = mine[tile, parity] + from_pair[tile]
        for hop in range(1, line):
            line_copy(tile, hop).start()

    @pl.when(step >= LAG)
    def _():
        tile = step - LAG
        total = half[tile, place]
        for hop in range(1, line):
            line_copy(tile, hop).wait_recv()
            total = total + from_line[tile, hop - 1]
        cols = pl.ds(pl.multiple_of(tile * span, span), span)
        scale = scale_ref[pl.ds(pl.multiple_of(me * own, own), own), :][:, :1]
        out_ref[:, cols] = total * scale * gain_ref[:, cols]
        pair_copy(tile).wait_send()
        for hop in range(1, line):
            line_copy(tile, hop).wait_send()


def product_and_sum(all_quant, down_int, gain, tensor_count, tokens):
    depth, columns = down_int.shape
    span = min(512, columns)
    tiles = columns // span
    line = tensor_count // 2
    own = tokens // tensor_count
    return pl.pallas_call(
        functools.partial(product_kernel, tiles),
        grid=(tiles + LAG,),
        out_shape=[
            jax.ShapeDtypeStruct((own, columns), jnp.float32),
            jax.ShapeDtypeStruct((tokens, LANES), jnp.float32),
        ],
        in_specs=[
            pl.BlockSpec(memory_space=pltpu.VMEM),
            pl.BlockSpec((depth, span), lambda i: (0, jnp.minimum(i, tiles - 1))),
            pl.BlockSpec(memory_space=pltpu.VMEM),
        ],
        out_specs=[pl.BlockSpec(memory_space=pltpu.VMEM)] * 2,
        scratch_shapes=[
            pltpu.VMEM((tiles, 2, line, own, span), jnp.float32),
            pltpu.VMEM((tiles, line, own, span), jnp.float32),
            pltpu.VMEM((tiles, line, own, span), jnp.float32),
            pltpu.VMEM((tiles, line - 1, own, span), jnp.float32),
            pltpu.SemaphoreType.DMA((tiles,)),
            pltpu.SemaphoreType.DMA((tiles,)),
            pltpu.SemaphoreType.DMA((tiles, line - 1)),
            pltpu.SemaphoreType.DMA((tiles, line - 1)),
        ],
        compiler_params=pltpu.CompilerParams(
            collective_id=0, has_side_effects=True, vmem_limit_bytes=60 * 1024 * 1024
        ),
        cost_estimate=pl.CostEstimate(
            flops=4 * tokens * depth * columns, bytes_accessed=2 * depth * columns, transcendentals=0
        ),
        name="product_and_sum",
    )(all_quant, down_int, gain)


def local(hidden, down_int, w_scale, had_small):
    tensor_count = lax.axis_size("tensor")
    seq_count = lax.axis_size("seq")
    tokens_here, units_here = hidden.shape
    had = had_small.shape[0]
    units = units_here * tensor_count
    rows = tokens_here // tensor_count
    parts = rows // ROWS
    group = LANES // math.gcd(had, LANES)
    width = group * had
    inner = units_here // width
    norm_factor = 1.0 / math.sqrt(units)

    factor = inner_factor(had_small, group)
    gathered = lax.all_to_all(
        hidden.reshape(tensor_count, rows, units_here), "tensor", split_axis=0, concat_axis=0, tiled=True
    ).reshape(tokens_here, units_here)
    quants = pl.pallas_call(
        functools.partial(rotate_kernel, tensor_count, rows, norm_factor),
        out_shape=[jax.ShapeDtypeStruct((tensor_count * 2 * ROWS, units_here + LANES), jnp.bfloat16)] * parts,
        in_specs=[pl.BlockSpec(memory_space=pltpu.VMEM)] * 2,
        out_specs=[pl.BlockSpec(memory_space=pltpu.VMEM)] * parts,
        scratch_shapes=[pltpu.VMEM((inner, tokens_here, width), jnp.float32)],
        compiler_params=pltpu.CompilerParams(vmem_limit_bytes=40 * 1024 * 1024),
        cost_estimate=pl.CostEstimate(
            flops=2 * inner * tokens_here * width * width,
            bytes_accessed=6 * tokens_here * units_here + 2 * width * width,
            transcendentals=0,
        ),
        name="rotate",
    )(gathered, factor)

    total_tokens = tokens_here * seq_count
    own_rows = total_tokens // tensor_count
    outs, scales = [], []
    for quant in quants:
        returned = lax.all_to_all(
            quant.reshape(tensor_count, 2 * ROWS, -1), "tensor", split_axis=0, concat_axis=0, tiled=True
        ).reshape(tensor_count * 2 * ROWS, -1)
        all_quant = lax.all_gather(returned, "seq", axis=0, tiled=True)
        summed, scale = product_and_sum(
            all_quant, down_int, w_scale[None, :], tensor_count, total_tokens // parts
        )
        outs.append(summed.reshape(own_rows // rows, ROWS, -1))
        offset = lax.axis_index("seq") * (tokens_here // parts)
        here = lax.dynamic_slice_in_dim(scale, offset, tokens_here // parts, 0)
        scales.append(here.reshape(tensor_count, ROWS, LANES))
    mixed = jnp.stack(outs, axis=1).reshape(own_rows, -1).astype(jnp.bfloat16)
    act_scale = jnp.stack(scales, axis=1).reshape(tokens_here, LANES)[:, 0]
    return (mixed, act_scale)


def solution(mesh):
    return jax.shard_map(
        local,
        mesh=mesh,
        in_specs=(P("seq", "tensor"), P("tensor", "seq"), P("seq"), P()),
        out_specs=(P("tensor", "seq"), P("seq")),
        check_vma=False,
    )
```

profile of v0, /device:TPU:0, one launch (start us, length us, event | category | flops | bytes accessed | tf_op | source)
XLA Modules:
  0.0 301.4 jit_solution(1156294865318243432)
XLA Ops:
  7.2 7.3 %all-to-all-start = ((bf16[8,16,6656]{2,1,0:T(8,128)(2,1)}), bf16[8,16,6656]{2,1,0:T(8,128)(2,1)S(1)}, u32[]{:S(2)}, u32[]{:S(2)}) async-start(bf16[8,16,6656]{2,1,0:T(8,128)(2,1)} %bitcast.22), calls=%async_computation | async-start | bytes 3407872 | tf_op jit(solution)/shard_map/all_to_all | solution.py:242
  14.5 0.0 all-gather.5.cloned.1.call-start
  14.5 12.1 %fusion.9.k_ref = bf16[1664,1664]{1,0:T(8,128)(2,1)} fusion(s32[1664]{0:T(1024)S(1)} %get-tuple-element.14, s32[1664]{0:T(1024)S(1)} %get-tuple-element.15, s32[1664]{0:T(1024)S(1)} %fusion.23, pred[1664]{0:T(1024)(128)(4,1)S(1)} %fusion.27, s32[52,52]{1,0:T(8,128)} %param.7), kind=kOutput, calls=%fused_computation.14 | convolution fusion | flops 352777344 | bytes 5570240 | tf_op jit(solution)/shard_map/dot_general | solution.py:35
  26.7 27.6 %all-to-all-done = bf16[8,16,6656]{2,1,0:T(8,128)(2,1)S(1)} async-done(((bf16[8,16,6656]{2,1,0:T(8,128)(2,1)}), bf16[8,16,6656]{2,1,0:T(8,128)(2,1)S(1)}, u32[]{:S(2)}, u32[]{:S(2)}) %all-to-all-start) | async-done | bytes 1703968 | tf_op jit(solution)/shard_map/all_to_all | solution.py:242
  54.3 0.0 copy-start
  54.3 2.6 copy-done
  56.8 6.1 %rotate.1 = (bf16[128,6784]{1,0:T(8,128)(2,1)S(1)}, bf16[128,6784]{1,0:T(8,128)(2,1)S(1)}) custom-call(bf16[128,6656]{1,0:T(8,128)(2,1)S(1)} %bitcast.19, bf16[1664,1664]{1,0:T(8,128)(2,1)S(1)} %copy-done), custom_call_target="tpu_custom_call" | custom-call | flops 2835349504 | bytes 10649600 | tf_op jit(solution)/shard_map/rotate/pallas_call | solution.py:245
  62.9 44.4 %all_to_all.15 = bf16[8,16,6784]{2,1,0:T(8,128)(2,1)} all-to-all(bf16[8,16,6784]{2,1,0:T(8,128)(2,1)S(1)} %bitcast.18), channel_id=1, replica_groups=mesh['seq'=4,'tensor'=8] {'tensor'}, dimensions={0} | all-to-all | bytes 3473408 | tf_op jit(solution)/shard_map/all_to_all | solution.py:264
  107.4 0.0 all-gather.5.cloned.1.call-update
  107.4 0.0 all-gather.3.cloned.1.call-start
  107.4 43.8 %all_to_all.16 = bf16[8,16,6784]{2,1,0:T(8,128)(2,1)} all-to-all(bf16[8,16,6784]{2,1,0:T(8,128)(2,1)S(1)} %bitcast.17), channel_id=1, replica_groups=mesh['seq'=4,'tensor'=8] {'tensor'}, dimensions={0} | all-to-all | bytes 3473408 | tf_op jit(solution)/shard_map/all_to_all | solution.py:264
  151.3 0.0 all-gather.3.cloned.1.call-update
  151.3 5.2 %all-gather.5.cloned.1.call-done.x_ref = bf16[512,6784]{1,0:T(8,128)(2,1)} async-done(((bf16[128,6784]{1,0:T(8,128)(2,1)}), bf16[512,6784]{1,0:T(8,128)(2,1)}) %all-gather.5.cloned.1.call-update) | async-done | bytes 6946832 | tf_op jit(solution)/shard_map/all_gather | solution.py:267
  156.5 66.9 %product_and_sum.3 = (f32[32,4096]{1,0:T(8,128)}, f32[256,128]{1,0:T(8,128)}) custom-call(bf16[512,6784]{1,0:T(8,128)(2,1)} %all-gather.5.cloned.1.call-done.x_ref, bf16[6656,4096]{1,0:T(8,128)(2,1)} %w_ref.3, f32[1,4096]{1,0:T(1,128)} %bitcast.25), custom_call_target="tpu_custom_call" | custom-call | flops 27917287424 | bytes 54525952 | tf_op jit(solution)/shard_map/product_and_sum/pallas_call | solution.py:195
  223.4 1.1 convert_bitcast_fusion
  224.5 0.0 all-gather.3.cloned.1.call-done.x_ref
  224.5 66.0 %product_and_sum.2 = (f32[32,4096]{1,0:T(8,128)}, f32[256,128]{1,0:T(8,128)}) custom-call(bf16[512,6784]{1,0:T(8,128)(2,1)} %all-gather.3.cloned.1.call-done.x_ref, bf16[6656,4096]{1,0:T(8,128)(2,1)} %w_ref.3, f32[1,4096]{1,0:T(1,128)} %bitcast.26), custom_call_target="tpu_custom_call" | custom-call | flops 27917287424 | bytes 54525952 | tf_op jit(solution)/shard_map/product_and_sum/pallas_call | solution.py:195
  290.5 1.1 convert_bitcast_fusion.1
  291.5 0.1 pad_maximum_fusion
  291.6 0.8 copy.9
  292.4 0.8 dynamic-slice_bitcast_fusion
  293.2 0.8 dynamic-slice_bitcast_fusion.1
  294.0 0.6 slice_reduce_fusion
  (5 shorter events, 0.0 us)
Async XLA Ops:
  7.2 47.1 %all-to-all-start = ((bf16[8,16,6656]{2,1,0:T(8,128)(2,1)}), bf16[8,16,6656]{2,1,0:T(8,128)(2,1)S(1)}, u32[]{:S(2)}, u32[]{:S(2)}) async-start(bf16[8,16,6656]{2,1,0:T(8,128)(2,1)} %bitcast.22), calls=%async_computation | async-start | bytes 3407872 | tf_op jit(solution)/shard_map/all_to_all | solution.py:242
  14.5 142.0 %all-gather.5.cloned.1.call-start = ((), (), s32[]{:S(2)}) async-start(), calls=%async_computation.4 | async-start | bytes 8683520 | tf_op jit(solution)/shard_map/all_gather | solution.py:267
  54.3 2.6 copy-start
  107.4 117.1 %all-gather.3.cloned.1.call-start = ((), (), s32[]{:S(2)}) async-start(), calls=%async_computation.3 | async-start | bytes 8683520 | tf_op jit(solution)/shard_map/all_gather | solution.py:267
Sparse Core Ops, SparseCore 0:
  107.5 48.8 all-gather.4
  158.0 50.0 all-gather.2
where the time goes:
time: 302 us; the launch traced here: 301 us
  Pallas kernels  139 us (46%)
  blocking collectives  88.3 us (29%)
  waiting for transfers between devices  32.8 us (11%)
  between operations  14.1 us (5%)
  matrix products  12.1 us (4%)
  starting transfers between devices  7.37 us (2%)
  local copies, waits for them, and re-layouts  5.55 us (2%)
    pallas_call x2, Pallas kernels, product_and_sum(): pl.pallas_call(functools.partial(product_kernel, tiles), grid=(tiles + LA...  133 us
    all_to_all x2, blocking collectives, local(): lax.all_to_all(quant.reshape(tensor_count, 2 * ROWS, -1), 'tensor', split...  88.3 us
    all_to_all x1, waiting for transfers between devices, local(): lax.all_to_all(hidden.reshape(tensor_count, rows, units_here), 'tensor',...  27.6 us
    dot_general x1, matrix products, inner_factor(): lax.dot_general(tall.astype(jnp.bfloat16), pick, (((1,), (1,)), ((), ()))...  12.1 us
    all_to_all x1, starting transfers between devices, local(): lax.all_to_all(hidden.reshape(tensor_count, rows, units_here), 'tensor',...  7.29 us
    pallas_call x1, Pallas kernels, local(): pl.pallas_call(functools.partial(rotate_kernel, tensor_count, rows, norm_...  6.09 us
  transfers between devices with their start and end apart: 3, of which 2 were waited for; matrix products, arithmetic and copies ran while one was open for 4% of the time, Pallas kernels for 22%

commit v1 on v0

--- a/solution.py
+++ b/solution.py
@@ -188,7 +188,7 @@
 
 def product_and_sum(all_quant, down_int, gain, tensor_count, tokens):
     depth, columns = down_int.shape
-    span = min(512, columns)
+    span = min(256, columns)
     tiles = columns // span
     line = tensor_count // 2
     own = tokens // tensor_count

time: 302 us -> 308 us (1.020)
  Pallas kernels: 139 us -> 145 us
    pallas_call x2, Pallas kernels: 133 us -> 139 us  [product_and_sum(): pl.pallas_call(functools.partial(product_kernel, tiles), grid=(tiles + LA...]
  transfers between devices with their start and end apart: 3 -> 3, of which waited for: 2 -> 2; matrix products, arithmetic and copies ran while one was open for 4% -> 4% of each run, Pallas kernels for 22% -> 23%
where the time goes in v1:
time: 308 us; the launch traced here: 307 us
  Pallas kernels  145 us (47%)
  blocking collectives  88.3 us (29%)
  waiting for transfers between devices  32.8 us (11%)
  between operations  14.1 us (5%)
  matrix products  12.1 us (4%)
  starting transfers between devices  7.37 us (2%)
  local copies, waits for them, and re-layouts  5.55 us (2%)
    pallas_call x2, Pallas kernels, product_and_sum(): pl.pallas_call(functools.partial(product_kernel, tiles), grid=(tiles + LA...  139 us
    all_to_all x2, blocking collectives, local(): lax.all_to_all(quant.reshape(tensor_count, 2 * ROWS, -1), 'tensor', split...  88.3 us
    all_to_all x1, waiting for transfers between devices, local(): lax.all_to_all(hidden.reshape(tensor_count, rows, units_here), 'tensor',...  27.6 us
    dot_general x1, matrix products, inner_factor(): lax.dot_general(tall.astype(jnp.bfloat16), pick, (((1,), (1,)), ((), ()))...  12.1 us
    all_to_all x1, starting transfers between devices, local(): lax.all_to_all(hidden.reshape(tensor_count, rows, units_here), 'tensor',...  7.29 us
  transfers between devices with their start and end apart: 3, of which 2 were waited for; matrix products, arithmetic and copies ran while one was open for 4% of the time, Pallas kernels for 23%

profile of v1, /device:TPU:0, one launch (start us, length us, event | category | flops | bytes accessed | tf_op | source)
XLA Modules:
  0.0 307.4 jit_solution(7711818774230439398)
XLA Ops:
  7.2 7.3 %all-to-all-start = ((bf16[8,16,6656]{2,1,0:T(8,128)(2,1)}), bf16[8,16,6656]{2,1,0:T(8,128)(2,1)S(1)}, u32[]{:S(2)}, u32[]{:S(2)}) async-start(bf16[8,16,6656]{2,1,0:T(8,128)(2,1)} %bitcast.22), calls=%async_computation | async-start | bytes 3407872 | tf_op jit(solution)/shard_map/all_to_all | solution.py:242
  14.5 0.0 all-gather.5.cloned.1.call-start
  14.5 12.1 %fusion.9.k_ref = bf16[1664,1664]{1,0:T(8,128)(2,1)} fusion(s32[1664]{0:T(1024)S(1)} %get-tuple-element.14, s32[1664]{0:T(1024)S(1)} %get-tuple-element.15, s32[1664]{0:T(1024)S(1)} %fusion.23, pred[1664]{0:T(1024)(128)(4,1)S(1)} %fusion.27, s32[52,52]{1,0:T(8,128)} %param.7), kind=kOutput, calls=%fused_computation.14 | convolution fusion | flops 352777344 | bytes 5570240 | tf_op jit(solution)/shard_map/dot_general | solution.py:35
  26.7 27.6 %all-to-all-done = bf16[8,16,6656]{2,1,0:T(8,128)(2,1)S(1)} async-done(((bf16[8,16,6656]{2,1,0:T(8,128)(2,1)}), bf16[8,16,6656]{2,1,0:T(8,128)(2,1)S(1)}, u32[]{:S(2)}, u32[]{:S(2)}) %all-to-all-start) | async-done | bytes 1703968 | tf_op jit(solution)/shard_map/all_to_all | solution.py:242
  54.3 0.0 copy-start
  54.3 2.6 copy-done
  56.8 6.1 %rotate.1 = (bf16[128,6784]{1,0:T(8,128)(2,1)S(1)}, bf16[128,6784]{1,0:T(8,128)(2,1)S(1)}) custom-call(bf16[128,6656]{1,0:T(8,128)(2,1)S(1)} %bitcast.19, bf16[1664,1664]{1,0:T(8,128)(2,1)S(1)} %copy-done), custom_call_target="tpu_custom_call" | custom-call | flops 2835349504 | bytes 10649600 | tf_op jit(solution)/shard_map/rotate/pallas_call | solution.py:245
  62.9 44.4 %all_to_all.15 = bf16[8,16,6784]{2,1,0:T(8,128)(2,1)} all-to-all(bf16[8,16,6784]{2,1,0:T(8,128)(2,1)S(1)} %bitcast.18), channel_id=1, replica_groups=mesh['seq'=4,'tensor'=8] {'tensor'}, dimensions={0} | all-to-all | bytes 3473408 | tf_op jit(solution)/shard_map/all_to_all | solution.py:264
  107.4 0.0 all-gather.5.cloned.1.call-update
  107.4 0.0 all-gather.3.cloned.1.call-start
  107.4 43.8 %all_to_all.16 = bf16[8,16,6784]{2,1,0:T(8,128)(2,1)} all-to-all(bf16[8,16,6784]{2,1,0:T(8,128)(2,1)S(1)} %bitcast.17), channel_id=1, replica_groups=mesh['seq'=4,'tensor'=8] {'tensor'}, dimensions={0} | all-to-all | bytes 3473408 | tf_op jit(solution)/shard_map/all_to_all | solution.py:264
  151.3 0.0 all-gather.3.cloned.1.call-update
  151.3 5.2 %all-gather.5.cloned.1.call-done.x_ref = bf16[512,6784]{1,0:T(8,128)(2,1)} async-done(((bf16[128,6784]{1,0:T(8,128)(2,1)}), bf16[512,6784]{1,0:T(8,128)(2,1)}) %all-gather.5.cloned.1.call-update) | async-done | bytes 6946832 | tf_op jit(solution)/shard_map/all_gather | solution.py:267
  156.5 69.5 %product_and_sum.3 = (f32[32,4096]{1,0:T(8,128)}, f32[256,128]{1,0:T(8,128)}) custom-call(bf16[512,6784]{1,0:T(8,128)(2,1)} %all-gather.5.cloned.1.call-done.x_ref, bf16[6656,4096]{1,0:T(8,128)(2,1)} %w_ref.3, f32[1,4096]{1,0:T(1,128)} %bitcast.25), custom_call_target="tpu_custom_call" | custom-call | flops 27917287424 | bytes 54525952 | tf_op jit(solution)/shard_map/product_and_sum/pallas_call | solution.py:195
  226.0 1.1 convert_bitcast_fusion
  227.0 0.0 all-gather.3.cloned.1.call-done.x_ref
  227.1 69.3 %product_and_sum.2 = (f32[32,4096]{1,0:T(8,128)}, f32[256,128]{1,0:T(8,128)}) custom-call(bf16[512,6784]{1,0:T(8,128)(2,1)} %all-gather.3.cloned.1.call-done.x_ref, bf16[6656,4096]{1,0:T(8,128)(2,1)} %w_ref.3, f32[1,4096]{1,0:T(1,128)} %bitcast.26), custom_call_target="tpu_custom_call" | custom-call | flops 27917287424 | bytes 54525952 | tf_op jit(solution)/shard_map/product_and_sum/pallas_call | solution.py:195
  296.4 1.1 convert_bitcast_fusion.1
  297.5 0.1 pad_maximum_fusion
  297.5 0.8 copy.9
  298.3 0.8 dynamic-slice_bitcast_fusion
  299.1 0.8 dynamic-slice_bitcast_fusion.1
  299.9 0.6 slice_reduce_fusion
  (5 shorter events, 0.0 us)
Async XLA Ops:
  7.2 47.1 %all-to-all-start = ((bf16[8,16,6656]{2,1,0:T(8,128)(2,1)}), bf16[8,16,6656]{2,1,0:T(8,128)(2,1)S(1)}, u32[]{:S(2)}, u32[]{:S(2)}) async-start(bf16[8,16,6656]{2,1,0:T(8,128)(2,1)} %bitcast.22), calls=%async_computation | async-start | bytes 3407872 | tf_op jit(solution)/shard_map/all_to_all | solution.py:242
  14.5 142.0 %all-gather.5.cloned.1.call-start = ((), (), s32[]{:S(2)}) async-start(), calls=%async_computation.4 | async-start | bytes 8683520 | tf_op jit(solution)/shard_map/all_gather | solution.py:267
  54.3 2.6 copy-start
  107.4 119.7 %all-gather.3.cloned.1.call-start = ((), (), s32[]{:S(2)}) async-start(), calls=%async_computation.3 | async-start | bytes 8683520 | tf_op jit(solution)/shard_map/all_gather | solution.py:267
Sparse Core Ops, SparseCore 0:
  107.5 48.8 all-gather.4
  158.0 50.0 all-gather.2
